TPU v7x, 1024 devices: a whole 4x4x32 slice. The times are simulated.
1024 devices in a mesh: expert: 64 (over z_lo, x), fsdp: 16 (over z_hi, y, core).
Axes of the slice: x: 4, y: 4, z: 32 (z_hi: 2, z_lo: 16; z = z_hi * 16 + z_lo), core: 2. Of those that a mesh axis runs over, the one named last changes fastest.
Arguments:
- tokens: bfloat16 [16384, 7168], P('expert', 'fsdp'), may hold values from -6 to 6
- output_grad: bfloat16 [16384, 7168], P('expert', 'fsdp'), may hold values from -6 to 6
- route_weight: float32 [16384, 8], P('expert'), may hold values from 0.05 to 0.5
- expert_ids: int32 [16384, 8], P('expert'), may hold values from 0 to 255, all different within a row; in each aligned block of 256 rows (0 to 255, 256 to 511, ...) at most 12 rows name the same one
- gate_weight: bfloat16 [64, 7168, 512], P('expert', 'fsdp'), may hold values from -0.0625 to 0.0625
- up_weight: bfloat16 [64, 7168, 512], P('expert', 'fsdp'), may hold values from -0.0625 to 0.0625
- down_weight: bfloat16 [64, 512, 7168], P('expert', None, 'fsdp'), may hold values from -0.1875 to 0.1875
Outputs:
- token_grad: bfloat16 [16384, 7168], P('expert', 'fsdp')
- gate_grad: bfloat16 [64, 7168, 512], P('expert', 'fsdp')
- up_grad: bfloat16 [64, 7168, 512], P('expert', 'fsdp')
- down_grad: bfloat16 [64, 512, 7168], P('expert', None, 'fsdp')
Inputs may be any that keep to these rules, and one draw needn't show every extreme that they name: `expert_ids`: in each block of 256 rows (the tokens held by one position along `expert` (one block of 256 consecutive rows)) no expert is named by more than 12 rows, a bound that some block reaches.
All inputs are finite; a program needn't handle non-finite values.
Results may differ from a plain program's by a relative error of at most 0.025.
Values may be sent and summed in bfloat16 or wider, within the bound.
A program may use at most 32 MiB of HBM per device.

v0:
```python
import jax
import jax.numpy as jnp
from jax import lax
from jax.sharding import PartitionSpec as P

CAP = 12


def swiglu_grads(gate, up_value, hidden_grad):
    sigmoid_gate = jax.nn.sigmoid(gate)
    activation = (gate * sigmoid_gate * up_value).astype(jnp.bfloat16)
    gate_delta = (
        hidden_grad * up_value * sigmoid_gate * (1.0 + gate * (1.0 - sigmoid_gate))
    ).astype(jnp.bfloat16)
    up_delta = (hidden_grad * gate * sigmoid_gate).astype(jnp.bfloat16)
    return (activation, gate_delta, up_delta)


def body(tokens, output_grad, route_weight, expert_ids, gate_weight, up_weight, down_weight):
    expert_count = lax.axis_size("expert")
    window = expert_count // 2
    tok_rows, top_count = expert_ids.shape
    slab_width = tokens.shape[1]
    slot_count = expert_count * CAP
    send_count = window * CAP
    in_window = expert_ids < window
    expert_hits = (
        expert_ids[:, :, None] == jnp.arange(window, dtype=jnp.int32)[None, None, :]
    ).astype(jnp.int32)
    flat_hits = expert_hits.reshape(tok_rows * top_count, window)
    earlier = jnp.cumsum(flat_hits, axis=0) - flat_hits
    slot_rank = jnp.sum(earlier * flat_hits, axis=1).reshape(tok_rows, top_count)
    slot_ids = jnp.where(in_window, expert_ids * CAP + slot_rank, -1)
    matches = slot_ids[None, :, :] == jnp.arange(send_count, dtype=jnp.int32)[:, None, None]
    placing = jnp.sum(matches.astype(jnp.float32), axis=2).astype(jnp.bfloat16)
    weighted = jnp.sum(jnp.where(matches, route_weight[None, :, :], 0.0), axis=2)
    sent_rows = jnp.dot(placing, tokens, preferred_element_type=jnp.float32).astype(jnp.bfloat16)
    sent_grads = jnp.dot(
        weighted, output_grad.astype(jnp.float32), precision=lax.Precision.HIGHEST
    ).astype(jnp.bfloat16)
    paired_rows = jnp.repeat(sent_rows.reshape(window, CAP, slab_width), 2, axis=0)
    paired_grads = jnp.repeat(sent_grads.reshape(window, CAP, slab_width), 2, axis=0)
    recv_rows, recv_grads = (
        lax.all_to_all(paired_rows, "expert", split_axis=0, concat_axis=0, tiled=True),
        lax.all_to_all(paired_grads, "expert", split_axis=0, concat_axis=0, tiled=True),
    )
    rows = recv_rows.reshape(slot_count, slab_width)
    grads = recv_grads.reshape(slot_count, slab_width)
    gate_w = gate_weight[0]
    up_w = up_weight[0]
    down_w = down_weight[0]
    hidden_width = gate_w.shape[1]
    over_rows = (((0,), (0,)), ((), ()))
    over_columns = (((1,), (1,)), ((), ()))
    gate_part = jnp.dot(rows, gate_w, preferred_element_type=jnp.float32)
    up_part = jnp.dot(rows, up_w, preferred_element_type=jnp.float32)
    hidden_part = lax.dot_general(grads, down_w, over_columns, preferred_element_type=jnp.float32)
    gate_sum, up_sum = (
        lax.psum(gate_part.astype(jnp.bfloat16), "fsdp").astype(jnp.float32),
        lax.psum(up_part.astype(jnp.bfloat16), "fsdp").astype(jnp.float32),
    )
    hidden_share = lax.psum_scatter(
        hidden_part.astype(jnp.bfloat16), "fsdp", scatter_dimension=1, tiled=True
    ).astype(jnp.float32)
    share_width = hidden_width // lax.axis_size("fsdp")
    share_start = lax.axis_index("fsdp") * share_width
    gate_share = lax.dynamic_slice_in_dim(gate_sum, share_start, share_width, 1)
    up_share = lax.dynamic_slice_in_dim(up_sum, share_start, share_width, 1)
    activation = (gate_sum * jax.nn.sigmoid(gate_sum) * up_sum).astype(jnp.bfloat16)
    unused, gate_piece, up_piece = swiglu_grads(gate_share, up_share, hidden_share)
    gate_delta, up_delta = (
        lax.all_gather(gate_piece, "fsdp", axis=1, tiled=True),
        lax.all_gather(up_piece, "fsdp", axis=1, tiled=True),
    )
    down_grad = lax.dot_general(
        activation, grads, over_rows, preferred_element_type=jnp.float32
    ).astype(jnp.bfloat16)
    gate_grad = lax.dot_general(
        rows, gate_delta, over_rows, preferred_element_type=jnp.float32
    ).astype(jnp.bfloat16)
    up_grad = lax.dot_general(rows, up_delta, over_rows, preferred_element_type=jnp.float32).astype(
        jnp.bfloat16
    )
    back_rows = lax.dot_general(
        gate_delta, gate_w, over_columns, preferred_element_type=jnp.float32
    )
    back_rows = (
        back_rows
        + lax.dot_general(up_delta, up_w, over_columns, preferred_element_type=jnp.float32)
    ).astype(jnp.bfloat16)
    returned = lax.all_to_all(
        back_rows.reshape(expert_count, CAP, slab_width),
        "expert",
        split_axis=0,
        concat_axis=0,
        tiled=True,
    )
    halves = returned.reshape(window, 2, CAP, slab_width)
    first_half = halves[:, 0].reshape(send_count, slab_width)
    second_half = halves[:, 1].reshape(send_count, slab_width)
    token_total = lax.dot_general(
        placing, first_half, over_rows, preferred_element_type=jnp.float32
    )
    token_total = token_total + lax.dot_general(
        placing, second_half, over_rows, preferred_element_type=jnp.float32
    )
    token_grad = token_total.astype(jnp.bfloat16)
    return (token_grad, gate_grad[None], up_grad[None], down_grad[None])


def solution(mesh):
    placed = (
        P("expert", "fsdp"),
        P("expert", "fsdp"),
        P("expert", None),
        P("expert", None),
        P("expert", "fsdp", None),
        P("expert", "fsdp", None),
        P("expert", None, "fsdp"),
    )
    return jax.shard_map(
        body,
        mesh=mesh,
        in_specs=placed,
        out_specs=(
            P("expert", "fsdp"),
            P("expert", "fsdp", None),
            P("expert", "fsdp", None),
            P("expert", None, "fsdp"),
        ),
        check_vma=False,
    )
```

profile of v0, /device:TPU:4, one launch (start us, length us, event | category | flops | bytes accessed | tf_op | source)
XLA Modules:
  0.0 1090.2 jit_solution(9603839030397210273)
XLA Ops:
  7.2 0.9 copy.49
  8.3 9.1 reduce-window.6
  18.4 2.6 convert_reduce_fusion
  21.7 1.1 broadcast_in_dim.40
  22.8 29.3 %all-to-all-start.1 = ((bf16[64,12,448]{2,1,0:T(8,128)(2,1)}), bf16[64,12,448]{2,1,0:T(8,128)(2,1)S(1)}, u32[]{:S(2)}, u32[]{:S(2)}) async-start(bf16[64,12,448]{2,1,0:T(8,128)(2,1)} %bitcast.5), calls=%async_computation.2 | async-start | bytes 2097152 | tf_op jit(solution)/shard_map/all_to_all | solution.py:44
  52.1 0.6 convolution_convert_fusion.7
  53.0 99.2 %all-to-all-done.1 = bf16[64,12,448]{2,1,0:T(8,128)(2,1)S(1)} async-done(((bf16[64,12,448]{2,1,0:T(8,128)(2,1)}), bf16[64,12,448]{2,1,0:T(8,128)(2,1)S(1)}, u32[]{:S(2)}, u32[]{:S(2)}) %all-to-all-start.1) | async-done | bytes 688160 | tf_op jit(solution)/shard_map/all_to_all | solution.py:44
  152.2 1.1 broadcast_in_dim.39
  153.3 12.8 %all-to-all-start = ((bf16[64,12,448]{2,1,0:T(8,128)(2,1)}), bf16[64,12,448]{2,1,0:T(8,128)(2,1)S(1)}, u32[]{:S(2)}, u32[]{:S(2)}) async-start(bf16[64,12,448]{2,1,0:T(8,128)(2,1)} %bitcast.68), calls=%async_computation | async-start | bytes 2097152 | tf_op jit(solution)/shard_map/all_to_all | solution.py:45
  166.2 0.4 reshape.62
  166.7 1.5 convolution_convert_fusion
  168.2 1.5 convolution_convert_fusion.1
  169.8 118.6 %all-to-all-done = bf16[64,12,448]{2,1,0:T(8,128)(2,1)S(1)} async-done(((bf16[64,12,448]{2,1,0:T(8,128)(2,1)}), bf16[64,12,448]{2,1,0:T(8,128)(2,1)S(1)}, u32[]{:S(2)}, u32[]{:S(2)}) %all-to-all-start) | async-done | bytes 688160 | tf_op jit(solution)/shard_map/all_to_all | solution.py:45
  288.3 0.4 reshape.59
  288.7 1.5 convolution_convert_fusion.2
  290.3 371.9 %all-reduce.3.cloned.1.call-done = (bf16[768,512]{0,1:T(8,128)(2,1)}, bf16[768,512]{0,1:T(8,128)(2,1)}) async-done(((bf16[768,512]{0,1:T(8,128)(2,1)}, bf16[768,512]{0,1:T(8,128)(2,1)}), (bf16[768,512]{0,1:T(8,128)(2,1)}, bf16[768,512]{0,1:T(8,128)(2,1)})) %all-reduce.3.cloned.1.call-update) | async-done | bytes 1572880 | tf_op jit(solution)/shard_map/psum | solution.py:60
  662.2 1.3 convert_element_type.72
  663.6 1.3 convert_element_type.74
  664.8 138.8 %reduce-scatter.2.cloned.1.call-done = bf16[768,32]{0,1:T(8,128)(2,1)} async-done(((bf16[768,512]{0,1:T(8,128)(2,1)}), bf16[768,32]{0,1:T(8,128)(2,1)}) %reduce-scatter.2.cloned.1.call-update) | async-done | bytes 49168 | tf_op jit(solution)/shard_map/reduce_scatter | solution.py:62
  803.6 1.0 fusion.21
  804.6 70.7 %all_gather.7 = bf16[768,512]{0,1:T(8,128)(2,1)S(1)} all-gather(bf16[768,32]{0,1:T(8,128)(2,1)S(1)} %get-tuple-element.8), channel_id=1, replica_groups=mesh['expert'=64,'fsdp'=16] {'fsdp'}, dimensions={1}, use_global_device_ids=true | all-gather | bytes 835584 | tf_op jit(solution)/shard_map/all_gather | solution.py:73
  875.3 72.3 %all_gather.6 = bf16[768,512]{0,1:T(8,128)(2,1)S(1)} all-gather(bf16[768,32]{0,1:T(8,128)(2,1)S(1)} %get-tuple-element.9), channel_id=1, replica_groups=mesh['expert'=64,'fsdp'=16] {'fsdp'}, dimensions={1}, use_global_device_ids=true | all-gather | bytes 835584 | tf_op jit(solution)/shard_map/all_gather | solution.py:72
  947.5 0.5 fusion.5
  948.1 1.4 fusion
  949.4 1.4 copy.58
  950.8 1.3 reshape.63
  952.1 28.8 %all-to-all-start.2 = ((bf16[64,12,448]{2,1,0:T(8,128)(2,1)}), bf16[64,12,448]{2,1,0:T(8,128)(2,1)S(1)}, u32[]{:S(2)}, u32[]{:S(2)}) async-start(bf16[64,12,448]{2,1,0:T(8,128)(2,1)} %reshape.63), calls=%async_computation.3 | async-start | bytes 2097152 | tf_op jit(solution)/shard_map/all_to_all | solution.py:91
  980.9 2.7 fusion.2
  983.6 1.4 fusion.1
  985.1 1.6 fusion.3
  986.6 94.9 %all-to-all-done.2 = bf16[64,12,448]{2,1,0:T(8,128)(2,1)S(1)} async-done(((bf16[64,12,448]{2,1,0:T(8,128)(2,1)}), bf16[64,12,448]{2,1,0:T(8,128)(2,1)S(1)}, u32[]{:S(2)}, u32[]{:S(2)}) %all-to-all-start.2) | async-done | bytes 688160 | tf_op jit(solution)/shard_map/all_to_all | solution.py:91
  1082.4 1.0 fusion.4
  (54 shorter events, 3.1 us)
Async XLA Ops:
  7.2 159.5 %copy-start = (bf16[1,448,512]{2,1,0:T(8,128)(2,1)S(1)}, bf16[1,448,512]{2,1,0:T(8,128)(2,1)}, u32[]{:S(2)}) copy-start(bf16[1,448,512]{2,1,0:T(8,128)(2,1)} %param.11) | copy-start | bytes 1376260
  7.2 11.2 %copy-start.12 = (s32[256,8]{0,1:T(8,128)S(1)}, s32[256,8]{0,1:T(8,128)}, u32[]{:S(2)}) copy-start(s32[256,8]{0,1:T(8,128)} %param.10) | copy-start | bytes 24580
  7.2 11.2 %copy-start.13 = (f32[256,8]{0,1:T(8,128)S(1)}, f32[256,8]{0,1:T(8,128)}, u32[]{:S(2)}) copy-start(f32[256,8]{0,1:T(8,128)} %param.9) | copy-start | bytes 24580
  8.3 12.7 %copy-start.10 = (bf16[256,448]{0,1:T(8,128)(2,1)S(1)}, bf16[256,448]{0,1:T(8,128)(2,1)}, u32[]{:S(2)}) copy-start(bf16[256,448]{0,1:T(8,128)(2,1)} %param.7) | copy-start | bytes 688132
  21.6 30.4 %copy-start.11 = (bf16[256,448]{0,1:T(8,128)(2,1)S(1)}, bf16[256,448]{0,1:T(8,128)(2,1)}, u32[]{:S(2)}) copy-start(bf16[256,448]{0,1:T(8,128)(2,1)} %param.8) | copy-start | bytes 688132
  22.8 129.4 %all-to-all-start.1 = ((bf16[64,12,448]{2,1,0:T(8,128)(2,1)}), bf16[64,12,448]{2,1,0:T(8,128)(2,1)S(1)}, u32[]{:S(2)}, u32[]{:S(2)}) async-start(bf16[64,12,448]{2,1,0:T(8,128)(2,1)} %bitcast.5), calls=%async_computation.2 | async-start | bytes 2097152 | tf_op jit(solution)/shard_map/all_to_all | solution.py:44
  153.3 135.0 %all-to-all-start = ((bf16[64,12,448]{2,1,0:T(8,128)(2,1)}), bf16[64,12,448]{2,1,0:T(8,128)(2,1)S(1)}, u32[]{:S(2)}, u32[]{:S(2)}) async-start(bf16[64,12,448]{2,1,0:T(8,128)(2,1)} %bitcast.68), calls=%async_computation | async-start | bytes 2097152 | tf_op jit(solution)/shard_map/all_to_all | solution.py:45
  166.2 496.0 %all-reduce.3.cloned.1.call-start = ((), (), s32[]{:S(2)}) async-start(), calls=%async_computation.5 | async-start | bytes 3145728 | tf_op jit(solution)/shard_map/psum | solution.py:60
  166.6 3.0 copy-start.1
  166.6 1.5 copy-start.8
  169.7 119.0 %copy-start.14 = (bf16[1,512,448]{1,2,0:T(8,128)(2,1)S(1)}, bf16[1,512,448]{1,2,0:T(8,128)(2,1)}, u32[]{:S(2)}) copy-start(bf16[1,512,448]{1,2,0:T(8,128)(2,1)} %param.13) | copy-start | bytes 1376260
  169.7 633.9 %reduce-scatter.2.cloned.1.call-start = ((), (), s32[]{:S(2)}) async-start(), calls=%async_computation.4 | async-start | bytes 835584 | tf_op jit(solution)/shard_map/reduce_scatter | solution.py:62
  288.7 373.5 %copy-start.3 = (bf16[768,448]{1,0:T(8,128)(2,1)}, bf16[768,448]{1,0:T(8,128)(2,1)S(1)}, u32[]{:S(2)}) copy-start(bf16[768,448]{1,0:T(8,128)(2,1)S(1)} %reshape.59) | copy-start | bytes 2064388
  662.2 1.4 copy-start.6
  875.3 72.8 %copy-start.9 = (bf16[1,448,512]{2,1,0:T(8,128)(2,1)S(1)}, bf16[1,448,512]{2,1,0:T(8,128)(2,1)}, u32[]{:S(2)}) copy-start(bf16[1,448,512]{2,1,0:T(8,128)(2,1)} %param.12) | copy-start | bytes 1376260
  952.1 129.5 %all-to-all-start.2 = ((bf16[64,12,448]{2,1,0:T(8,128)(2,1)}), bf16[64,12,448]{2,1,0:T(8,128)(2,1)S(1)}, u32[]{:S(2)}, u32[]{:S(2)}) async-start(bf16[64,12,448]{2,1,0:T(8,128)(2,1)} %reshape.63), calls=%async_computation.3 | async-start | bytes 2097152 | tf_op jit(solution)/shard_map/all_to_all | solution.py:91
  980.9 2.7 copy-start.2
  980.9 4.1 copy-start.7
  983.6 1.4 copy-start.4
  983.6 1.4 copy-start.5
Sparse Core Ops, SparseCore 0:
  170.6 491.5 all-reduce.2
  669.0 134.6 reduce-scatter.1
where the time goes:
time: 1090 us
  waiting for transfers between devices  823 us (76%)
  blocking collectives  143 us (13%)
  starting transfers between devices  71 us (7%)
  other arithmetic  15.6 us (1%)
  between operations  14.4 us (1%)
  matrix products  14.3 us (1%)
    psum x1, waiting for transfers between devices, body(): lax.psum(up_part.astype(jnp.bfloat16), 'fsdp').astype(jnp.float32)  372 us
    reduce_scatter x1, waiting for transfers between devices, body(): lax.psum_scatter(hidden_part.astype(jnp.bfloat16), 'fsdp', scatter_dimens...  139 us
    all_to_all x1, waiting for transfers between devices, body(): lax.all_to_all(paired_grads, 'expert', split_axis=0, concat_axis=0, tiled...  119 us
    all_to_all x1, waiting for transfers between devices, body(): lax.all_to_all(paired_rows, 'expert', split_axis=0, concat_axis=0, tiled=...  99.2 us
    all_to_all x1, waiting for transfers between devices, body(): lax.all_to_all(back_rows.reshape(expert_count, CAP, slab_width), 'expert'...  94.9 us
    all_gather x1, blocking collectives, body(): lax.all_gather(gate_piece, 'fsdp', axis=1, tiled=True)  72.3 us
    all_gather x1, blocking collectives, body(): lax.all_gather(up_piece, 'fsdp', axis=1, tiled=True)  70.7 us
    all_to_all x1, starting transfers between devices, body(): lax.all_to_all(paired_rows, 'expert', split_axis=0, concat_axis=0, tiled=...  29.3 us
  transfers between devices with their start and end apart: 5, of which 5 were waited for; matrix products, arithmetic and copies ran while one was open for 1% of the time, Pallas kernels for 0%

commit v1 on v0

v1 whole, which is shorter than its diff:
```python
import jax
import jax.numpy as jnp
from jax import lax
from jax.experimental import pallas as pl
from jax.experimental.pallas import tpu as pltpu
from jax.sharding import PartitionSpec as P

MESH = pl.DeviceIdType.MESH
BF = jnp.bfloat16
F32 = jnp.float32
CAP = 12
NX = 4
NY = 4
CHUNKS = 4

NN = (((1,), (0,)), ((), ()))
NT = (((1,), (1,)), ((), ()))
TN = (((0,), (0,)), ((), ()))


def dot(a, b, dims=NN):
    return lax.dot_general(a, b, dims, preferred_element_type=F32)


def iota(shape, dim):
    return lax.broadcasted_iota(jnp.int32, shape, dim)


def make_kernel(nz, width):
    slots = 2 * CAP
    group = nz // CHUNKS
    span = group * CAP
    rows = NX * span
    low = 2 * width - 512

    def kernel(
        ids, rw, xg, w3, wd3,
        token_grad, gate_grad, up_grad, down_grad,
        placing, send, zrecv, xsend, held, part, crecv, ysend, yrecv, zsend, zhrecv,
        hid, back, bxrecv, zret, ret,
        za_s, za_r, xa_s, xa_r, ca_s, ca_r, ya_s, ya_r, zh_s, zh_r,
        yb_s, yb_r, cb_s, cb_r, xb_s, xb_r, zb_s, zb_r,
    ):
        ei, fi = lax.axis_index("expert"), lax.axis_index("fsdp")
        zl, x = ei // NX, ei % NX
        zh, y, core = fi // (2 * NY), (fi // 2) % NY, fi % 2

        def at_z(k):
            return (lax.rem(zl + k, nz) * NX + x, fi)

        def at_x(k):
            return (zl * NX + lax.rem(x + k, NX), fi)

        def at_y(k):
            return (ei, zh * 2 * NY + lax.rem(y + k, NY) * 2 + core)

        sibling = (ei, fi + 1 - 2 * core)
        across = (ei, lax.rem(fi + 2 * NY, 4 * NY))

        barrier = pltpu.get_barrier_semaphore()
        others = [at_z(k) for k in range(1, nz)] + [at_x(k) for k in range(1, NX)]
        others += [at_y(k) for k in range(1, NY)] + [sibling, across]
        for other in others:
            pl.semaphore_signal(barrier, inc=1, device_id=other, device_id_type=MESH)

        sent = []

        def copy(src, dst, s, r, to):
            c = pltpu.make_async_remote_copy(
                src_ref=src, dst_ref=dst, send_sem=s, recv_sem=r, device_id=to, device_id_type=MESH
            )
            c.start()
            sent.append(c)
            return c

        n_exp, n_tok = 2 * nz, xg.shape[0]
        n_slot = n_exp * CAP
        names = iota((n_exp, n_tok), 0)
        hits = jnp.zeros((n_exp, n_tok), F32)
        gains = jnp.zeros((n_exp, n_tok), F32)
        for k in range(ids.shape[0]):
            same = ids[k : k + 1, :] == names
            hits = hits + jnp.where(same, 1.0, 0.0)
            gains = gains + jnp.where(same, rw[k : k + 1, :], 0.0)
        before = jnp.where(iota((n_tok, n_tok), 0) < iota((n_tok, n_tok), 1), 1.0, 0.0).astype(BF)
        rank = dot(hits.astype(BF), before)
        rank = jnp.where(hits > 0.0, rank, -1.0).astype(BF)
        first = iota((n_slot, n_exp), 1) * CAP
        row = iota((n_slot, n_exp), 0)
        owner = jnp.where((row >= first) & (row < first + CAP), 1.0, 0.0)
        slot = jnp.sum(owner * (row - first).astype(F32), axis=1, keepdims=True)
        ranks = dot(owner.astype(BF), rank)
        chosen = ranks == slot
        placing[...] = jnp.where(chosen, 1.0, 0.0).astype(BF)
        gain = lax.dot_general(
            owner, gains, NN, precision=lax.Precision.HIGHEST, preferred_element_type=F32
        )
        gain = jnp.sum(jnp.where(chosen, gain, 0.0), axis=1, keepdims=True)
        placed = dot(placing[...], xg[...])
        scale = jnp.where(iota(placed.shape, 1) < width, 1.0, gain)
        send[...] = (placed * scale).astype(BF).reshape(send.shape)

        pl.semaphore_wait(barrier, len(others))

        za = {}
        for c in range(CHUNKS):
            for m in reversed(range(group)):
                k = c + CHUNKS * m
                if k == 0:
                    continue
                za[k] = copy(
                    send.at[lax.rem(zl + nz - k, nz)], zrecv.at[c * group + m],
                    za_s.at[k], za_r.at[k], at_z(nz - k),
                )
        zrecv[0] = send[zl]

        wide = group * slots
        to, fro = iota((wide, wide), 0), iota((wide, wide), 1)
        half = jnp.where(to >= span, 1, 0)
        rest = to - half * span
        shuffle = jnp.zeros((wide, wide), F32)
        for m in range(group):
            inside = (rest >= m * CAP) & (rest < (m + 1) * CAP)
            shuffle = shuffle + jnp.where(
                inside & (fro == rest - m * CAP + m * slots + half * CAP), 1.0, 0.0
            )
        shuffle = shuffle.astype(BF)

        def products(c):
            for m in range(group):
                if c + CHUNKS * m:
                    za[c + CHUNKS * m].wait_recv()
            slabs = zrecv[c * group : (c + 1) * group].reshape(wide, 2 * width)
            xsend[c] = dot(shuffle, slabs).astype(BF).reshape(2, span, 2 * width)
            xa = [
                copy(
                    xsend.at[c, lax.rem(x + j, NX) // 2], held.at[c, j],
                    xa_s.at[c, j], xa_r.at[c, j], at_x(j),
                )
                for j in range(1, NX)
            ]
            held[c, 0] = xsend[c, x // 2]
            for cp in xa:
                cp.wait_recv()
            mine = held[c].reshape(rows, 2 * width)

            def half_product(h):
                part[c, h, :, 0:512] = dot(mine[:, 0:512], w3[h]).astype(BF)
                part[c, h, :, 512:768] = dot(mine[:, low:], wd3[h], NT).astype(BF)

            half_product(1 - core)
            ca = copy(part.at[c, 1 - core], crecv.at[c], ca_s.at[c], ca_r.at[c], sibling)
            half_product(core)
            ca.wait_recv()
            both = part[c, core].astype(F32) + crecv[c].astype(F32)
            ysend[c] = both.astype(BF).reshape(NY, span, 768)
            ya = [
                copy(
                    ysend.at[c, lax.rem(y + j, NY)], yrecv.at[c, j - 1],
                    ya_s.at[c, j], ya_r.at[c, j], at_y(j),
                )
                for j in range(1, NY)
            ]
            total = ysend[c, y].astype(F32)
            for j in range(1, NY):
                ya[j - 1].wait_recv()
                total = total + yrecv[c, j - 1].astype(F32)
            zsend[c] = total.astype(BF)
            return copy(zsend.at[c], zhrecv.at[c], zh_s.at[c], zh_r.at[c], across)

        def gradients(c, zh_copy):
            zh_copy.wait_recv()
            total = zsend[c].astype(F32) + zhrecv[c].astype(F32)
            gate, up, hgrad = total[:, 0:256], total[:, 256:512], total[:, 512:768]
            sig = 1.0 / (1.0 + jnp.exp(-gate))
            hid[c, core, y, :, 0:256] = (gate * sig * up).astype(BF)
            hid[c, core, y, :, 256:512] = (hgrad * up * sig * (1.0 + gate * (1.0 - sig))).astype(BF)
            hid[c, core, y, :, 512:768] = (hgrad * gate * sig).astype(BF)
            yb = [
                copy(
                    hid.at[c, core, y], hid.at[c, core, y],
                    yb_s.at[c, j], yb_r.at[c, j], at_y(j),
                )
                for j in range(1, NY)
            ]
            for cp in yb:
                cp.wait_recv()
            cb = copy(hid.at[c, core], hid.at[c, core], cb_s.at[c], cb_r.at[c], sibling)
            own = dot(hid[c, core, :, :, 256:768].reshape(rows, 512), w3[core], NT)
            cb.wait_recv()
            own = own + dot(hid[c, 1 - core, :, :, 256:768].reshape(rows, 512), w3[1 - core], NT)
            back[c] = own[:, 0:width].astype(BF).reshape(NX, span, width)
            return [
                copy(
                    back.at[c, j], bxrecv.at[c, j], xb_s.at[c, j], xb_r.at[c, j], at_x(NX - j)
                )
                for j in range(1, NX)
            ]

        def give_back(c, xb):
            bxrecv[c, 0] = back[c, 0]
            for cp in xb:
                cp.wait_recv()
            pair = []
            for e in range(2):
                one = bxrecv[c, lax.rem(2 * e + NX - x, NX)].astype(F32)
                two = bxrecv[c, lax.rem(2 * e + 1 + NX - x, NX)].astype(F32)
                pair.append((one + two).astype(BF))
            slabs = dot(shuffle, jnp.concatenate(pair, axis=0), TN).astype(BF)
            zret[c] = slabs.reshape(group, slots, width)
            out = []
            for m in reversed(range(group)):
                k = c + CHUNKS * m
                if k == 0:
                    ret[zl] = zret[0, 0]
                    continue
                out.append(
                    copy(zret.at[c, m], ret.at[zl], zb_s.at[k], zb_r.at[k], at_z(k))
                )
            return out

        zb = []
        across_copies = [products(c) for c in range(CHUNKS)]
        for c in range(CHUNKS):
            zb += give_back(c, gradients(c, across_copies[c]))

        rows_all = held[...].reshape(CHUNKS * rows, 2 * width)
        for h in range(2):
            grads = hid[:, h, :, :, :].reshape(CHUNKS * rows, 768)
            gu = dot(rows_all[:, 0:512], grads[:, 256:768], TN).astype(BF)
            gate_grad[:, 256 * h : 256 * h + 256] = gu[0:width, 0:256]
            up_grad[:, 256 * h : 256 * h + 256] = gu[0:width, 256:512]
            down_grad[256 * h : 256 * h + 256, :] = dot(grads[:, 0:256], rows_all[:, low:], TN).astype(BF)

        for cp in zb:
            cp.wait_recv()
        token_grad[...] = dot(placing[...], ret[...].reshape(n_slot, width), TN).astype(BF)
        for cp in sent:
            cp.wait_send()

    return kernel


def body(tokens, output_grad, route_weight, expert_ids, gate_weight, up_weight, down_weight):
    nz = lax.axis_size("expert") // NX
    width = tokens.shape[1]
    hidden = gate_weight.shape[2]
    group = nz // CHUNKS
    span = group * CAP
    rows = NX * span
    n_slot = 2 * nz * CAP
    pad = 512 - width
    xg = jnp.concatenate([tokens, output_grad], axis=1)
    halves = [
        jnp.concatenate([gate_weight[0, :, h : h + 256], up_weight[0, :, h : h + 256]], axis=1)
        for h in (0, 256)
    ]
    w3 = jnp.pad(jnp.stack(halves), ((0, 0), (0, pad), (0, 0)))
    wd3 = jnp.pad(down_weight[0], ((0, 0), (pad, 0))).reshape(2, hidden // 2, 512)
    vmem = pl.BlockSpec(memory_space=pltpu.VMEM)

    def dma(*shape):
        return [pltpu.SemaphoreType.DMA(shape)] * 2

    token_grad, gate_grad, up_grad, down_grad = pl.pallas_call(
        make_kernel(nz, width),
        out_shape=(
            jax.ShapeDtypeStruct(tokens.shape, BF),
            jax.ShapeDtypeStruct((width, hidden), BF),
            jax.ShapeDtypeStruct((width, hidden), BF),
            jax.ShapeDtypeStruct((hidden, 512), BF),
        ),
        in_specs=[vmem] * 5,
        out_specs=(vmem,) * 4,
        scratch_shapes=[
            pltpu.VMEM((n_slot, tokens.shape[0]), BF),
            pltpu.VMEM((nz, 2 * CAP, 2 * width), BF),
            pltpu.VMEM((nz, 2 * CAP, 2 * width), BF),
            pltpu.VMEM((CHUNKS, 2, span, 2 * width), BF),
            pltpu.VMEM((CHUNKS, NX, span, 2 * width), BF),
            pltpu.VMEM((CHUNKS, 2, rows, 768), BF),
            pltpu.VMEM((CHUNKS, rows, 768), BF),
            pltpu.VMEM((CHUNKS, NY, span, 768), BF),
            pltpu.VMEM((CHUNKS, NY - 1, span, 768), BF),
            pltpu.VMEM((CHUNKS, span, 768), BF),
            pltpu.VMEM((CHUNKS, span, 768), BF),
            pltpu.VMEM((CHUNKS, 2, NY, span, 768), BF),
            pltpu.VMEM((CHUNKS, NX, span, width), BF),
            pltpu.VMEM((CHUNKS, NX, span, width), BF),
            pltpu.VMEM((CHUNKS, group, 2 * CAP, width), BF),
            pltpu.VMEM((nz, 2 * CAP, width), BF),
            *dma(nz), *dma(CHUNKS, NX), *dma(CHUNKS), *dma(CHUNKS, NY), *dma(CHUNKS),
            *dma(CHUNKS, NY), *dma(CHUNKS), *dma(CHUNKS, NX), *dma(nz),
        ],
        compiler_params=pltpu.CompilerParams(
            collective_id=1, has_side_effects=True, vmem_limit_bytes=56 * 2**20
        ),
        name="layer",
    )(expert_ids.T, route_weight.T, xg, w3, wd3)
    return token_grad, gate_grad[None], up_grad[None], down_grad[None, :, pad:]


def solution(mesh):
    rows, last = P("expert", "fsdp"), P("expert", None, "fsdp")
    weight = P("expert", "fsdp", None)
    return jax.shard_map(
        body,
        mesh=mesh,
        in_specs=(rows, rows, P("expert", None), P("expert", None), weight, weight, last),
        out_specs=(rows, weight, weight, last),
        check_vma=False,
    )
```

time: 1090 us -> 230 us (0.21)
  the two profiles are of different devices: /device:TPU:4 before, /device:TPU:98 now
where the time goes in v1:
time: 230 us; the launch traced here: 229 us
  Pallas kernels  217 us (94%)
  local copies, waits for them, and re-layouts  9.38 us (4%)
    pallas_call x1, Pallas kernels, body(): pl.pallas_call(make_kernel(nz, width), out_shape=(jax.ShapeDtypeStruct(to...  217 us
    unnamed x17, local copies, waits for them, and re-layouts  6.85 us

profile of v1, /device:TPU:98, one launch (start us, length us, event | category | flops | bytes accessed | tf_op | source)
XLA Modules:
  0.0 229.2 jit_solution(6936532952565361479)
XLA Ops:
  0.6 0.0 copy-start
  0.6 1.1 copy.11
  1.8 1.1 copy.12
  2.9 0.0 copy-start.1
  2.9 0.9 pad_maximum_fusion.xg
  3.8 0.0 copy-done
  3.8 0.1 copy-done.1
  3.9 0.1 maximum_bitcast_fusion
  4.0 0.0 copy-start.4
  4.0 1.0 fusion.2.w3
  5.0 0.1 copy-done.4
  5.1 0.2 copy.16
  5.3 1.1 pad.9.clone
  6.5 217.1 %layer.1 = (bf16[256,448]{1,0:T(8,128)(2,1)}, bf16[448,512]{1,0:T(8,128)(2,1)}, bf16[448,512]{1,0:T(8,128)(2,1)}, bf16[512,512]{1,0:T(8,128)(2,1)}) custom-call(s32[8,256]{1,0:T(8,128)} %bitcast.24, f32[8,256]{1,0:T(8,128)} %bitcast.25, bf16[256,896]{1,0:T(8,128)(2,1)} %pad_maximum_fusion.xg, bf16[2,512,512]{2,1,0:T(8,128)(2,1)} %fusion.2.w3, ...), custom_call_target="tpu_custom_call" | custom-call | tf_op jit(solution)/shard_map/layer/pallas_call | solution.py:265
  223.6 1.8 copy.14
  225.4 0.0 copy-start.3
  225.4 1.3 slice_bitcast_fusion
  226.7 0.0 copy-start.2
  226.7 1.0 copy.15
  227.7 0.0 copy-done.3
  227.7 0.8 copy.19
  228.5 0.0 copy-done.2
  228.5 0.8 copy.20
  (2 shorter events, 0.1 us)
Async XLA Ops:
  0.6 3.2 %copy-start = (bf16[1,448,512]{2,1,0:T(8,128)(2,1)S(1)}, bf16[1,448,512]{2,1,0:T(8,128)(2,1)}, u32[]{:S(2)}) copy-start(bf16[1,448,512]{2,1,0:T(8,128)(2,1)} %param.11) | copy-start | bytes 1376260
  2.9 1.0 copy-start.1
  4.0 1.1 copy-start.4
  225.4 2.3 %copy-start.3 = (bf16[448,512]{1,0:T(8,128)(2,1)S(1)}, bf16[448,512]{1,0:T(8,128)(2,1)}, u32[]{:S(2)}) copy-start(bf16[448,512]{1,0:T(8,128)(2,1)} %get-tuple-element.9) | copy-start | bytes 1376260
  226.7 1.7 copy-start.2

commit v2 on v1

--- a/solution.py
+++ b/solution.py
@@ -12,6 +12,7 @@
 NX = 4
 NY = 4
 CHUNKS = 4
+TURN = (0, 1, 2, 3)
 
 NN = (((1,), (0,)), ((), ()))
 NT = (((1,), (1,)), ((), ()))
@@ -34,9 +35,9 @@
     low = 2 * width - 512
 
     def kernel(
-        ids, rw, xg, w3, wd3,
+        ids, rw, tokens, output_grad, gate_w, up_w, down_w,
         token_grad, gate_grad, up_grad, down_grad,
-        placing, send, zrecv, xsend, held, part, crecv, ysend, yrecv, zsend, zhrecv,
+        xg, w3, wd3, placing, send, zrecv, xsend, held, part, crecv, ysend, yrecv, zsend, zhrecv,
         hid, back, bxrecv, zret, ret,
         za_s, za_r, xa_s, xa_r, ca_s, ca_r, ya_s, ya_r, zh_s, zh_r,
         yb_s, yb_r, cb_s, cb_r, xb_s, xb_r, zb_s, zb_r,
@@ -73,7 +74,7 @@
             sent.append(c)
             return c
 
-        n_exp, n_tok = 2 * nz, xg.shape[0]
+        n_exp, n_tok = 2 * nz, tokens.shape[1]
         n_slot = n_exp * CAP
         names = iota((n_exp, n_tok), 0)
         hits = jnp.zeros((n_exp, n_tok), F32)
@@ -96,22 +97,33 @@
             owner, gains, NN, precision=lax.Precision.HIGHEST, preferred_element_type=F32
         )
         gain = jnp.sum(jnp.where(chosen, gain, 0.0), axis=1, keepdims=True)
-        placed = dot(placing[...], xg[...])
+        xg[0:width] = tokens[...]
+        xg[width:] = output_grad[...]
+        placed = dot(placing[...], xg[...], NT)
         scale = jnp.where(iota(placed.shape, 1) < width, 1.0, gain)
         send[...] = (placed * scale).astype(BF).reshape(send.shape)
 
         pl.semaphore_wait(barrier, len(others))
 
         za = {}
-        for c in range(CHUNKS):
-            for m in reversed(range(group)):
-                k = c + CHUNKS * m
-                if k == 0:
-                    continue
-                za[k] = copy(
-                    send.at[lax.rem(zl + nz - k, nz)], zrecv.at[c * group + m],
-                    za_s.at[k], za_r.at[k], at_z(nz - k),
-                )
+
+        def away(k):
+            return min(k, nz - k)
+
+        def dispatch(g):
+            for k in sorted(range(1, nz), key=away, reverse=True):
+                if k % 4 == TURN[g]:
+                    za[k] = copy(
+                        send.at[lax.rem(zl + nz - k, nz)], zrecv.at[k % CHUNKS * group + k // CHUNKS],
+                        za_s.at[k], za_r.at[k], at_z(nz - k),
+                    )
+
+        def dispatched(g):
+            for k in za:
+                if k % 4 == TURN[g]:
+                    za[k].wait_send()
+                    sent.remove(za[k])
+
         zrecv[0] = send[zl]
 
         wide = group * slots
@@ -126,13 +138,15 @@
             )
         shuffle = shuffle.astype(BF)
 
-        def products(c):
+        xa, ca, ya, zx, yb, cb, xb, zb = {}, {}, {}, {}, {}, {}, {}, []
+
+        def spread(c):
             for m in range(group):
                 if c + CHUNKS * m:
                     za[c + CHUNKS * m].wait_recv()
             slabs = zrecv[c * group : (c + 1) * group].reshape(wide, 2 * width)
             xsend[c] = dot(shuffle, slabs).astype(BF).reshape(2, span, 2 * width)
-            xa = [
+            xa[c] = [
                 copy(
                     xsend.at[c, lax.rem(x + j, NX) // 2], held.at[c, j],
                     xa_s.at[c, j], xa_r.at[c, j], at_x(j),
@@ -140,66 +154,76 @@
                 for j in range(1, NX)
             ]
             held[c, 0] = xsend[c, x // 2]
-            for cp in xa:
+
+        def multiply(c):
+            for cp in xa[c]:
                 cp.wait_recv()
             mine = held[c].reshape(rows, 2 * width)
 
             def half_product(h):
                 part[c, h, :, 0:512] = dot(mine[:, 0:512], w3[h]).astype(BF)
-                part[c, h, :, 512:768] = dot(mine[:, low:], wd3[h], NT).astype(BF)
+                part[c, h, :, 512:768] = dot(mine[:, low:], wd3[h]).astype(BF)
 
             half_product(1 - core)
-            ca = copy(part.at[c, 1 - core], crecv.at[c], ca_s.at[c], ca_r.at[c], sibling)
+            ca[c] = copy(part.at[c, 1 - core], crecv.at[c], ca_s.at[c], ca_r.at[c], sibling)
             half_product(core)
-            ca.wait_recv()
+
+        def add_cores(c):
+            ca[c].wait_recv()
             both = part[c, core].astype(F32) + crecv[c].astype(F32)
             ysend[c] = both.astype(BF).reshape(NY, span, 768)
-            ya = [
+            ya[c] = [
                 copy(
                     ysend.at[c, lax.rem(y + j, NY)], yrecv.at[c, j - 1],
                     ya_s.at[c, j], ya_r.at[c, j], at_y(j),
                 )
                 for j in range(1, NY)
             ]
+
+        def add_columns(c):
             total = ysend[c, y].astype(F32)
             for j in range(1, NY):
-                ya[j - 1].wait_recv()
+                ya[c][j - 1].wait_recv()
                 total = total + yrecv[c, j - 1].astype(F32)
             zsend[c] = total.astype(BF)
-            return copy(zsend.at[c], zhrecv.at[c], zh_s.at[c], zh_r.at[c], across)
-
-        def gradients(c, zh_copy):
-            zh_copy.wait_recv()
+            zx[c] = copy(zsend.at[c], zhrecv.at[c], zh_s.at[c], zh_r.at[c], across)
+
+        def activate(c):
+            zx[c].wait_recv()
             total = zsend[c].astype(F32) + zhrecv[c].astype(F32)
             gate, up, hgrad = total[:, 0:256], total[:, 256:512], total[:, 512:768]
             sig = 1.0 / (1.0 + jnp.exp(-gate))
             hid[c, core, y, :, 0:256] = (gate * sig * up).astype(BF)
             hid[c, core, y, :, 256:512] = (hgrad * up * sig * (1.0 + gate * (1.0 - sig))).astype(BF)
             hid[c, core, y, :, 512:768] = (hgrad * gate * sig).astype(BF)
-            yb = [
+            yb[c] = [
                 copy(
                     hid.at[c, core, y], hid.at[c, core, y],
                     yb_s.at[c, j], yb_r.at[c, j], at_y(j),
                 )
                 for j in range(1, NY)
             ]
-            for cp in yb:
+
+        def gather(c):
+            for cp in yb[c]:
                 cp.wait_recv()
-            cb = copy(hid.at[c, core], hid.at[c, core], cb_s.at[c], cb_r.at[c], sibling)
+            cb[c] = copy(hid.at[c, core], hid.at[c, core], cb_s.at[c], cb_r.at[c], sibling)
+
+        def multiply_back(c):
             own = dot(hid[c, core, :, :, 256:768].reshape(rows, 512), w3[core], NT)
-            cb.wait_recv()
+            cb[c].wait_recv()
             own = own + dot(hid[c, 1 - core, :, :, 256:768].reshape(rows, 512), w3[1 - core], NT)
             back[c] = own[:, 0:width].astype(BF).reshape(NX, span, width)
-            return [
+            xb[c] = [
                 copy(
                     back.at[c, j], bxrecv.at[c, j], xb_s.at[c, j], xb_r.at[c, j], at_x(NX - j)
                 )
                 for j in range(1, NX)
             ]
-
-        def give_back(c, xb):
             bxrecv[c, 0] = back[c, 0]
-            for cp in xb:
+
+        def add_halves(c):
+            for cp in xb[c]:
                 cp.wait_recv()
             pair = []
             for e in range(2):
@@ -208,21 +232,36 @@
                 pair.append((one + two).astype(BF))
             slabs = dot(shuffle, jnp.concatenate(pair, axis=0), TN).astype(BF)
             zret[c] = slabs.reshape(group, slots, width)
-            out = []
+
+        def give_back(c):
             for m in reversed(range(group)):
                 k = c + CHUNKS * m
                 if k == 0:
                     ret[zl] = zret[0, 0]
                     continue
-                out.append(
-                    copy(zret.at[c, m], ret.at[zl], zb_s.at[k], zb_r.at[k], at_z(k))
-                )
-            return out
-
-        zb = []
-        across_copies = [products(c) for c in range(CHUNKS)]
-        for c in range(CHUNKS):
-            zb += give_back(c, gradients(c, across_copies[c]))
+                zb.append(copy(zret.at[c, m], ret.at[zl], zb_s.at[k], zb_r.at[k], at_z(k)))
+
+        def lay_weights(_):
+            for h in range(2):
+                w3[h, 0:width, 0:256] = gate_w[:, 256 * h : 256 * h + 256]
+                w3[h, 0:width, 256:512] = up_w[:, 256 * h : 256 * h + 256]
+                w3[h, width:, :] = jnp.zeros((512 - width, 512), BF)
+                wd3[h, 0 : 512 - width, :] = jnp.zeros((512 - width, 256), BF)
+                wd3[h, 512 - width :, :] = down_w[:, 256 * h : 256 * h + 256]
+
+        order = (
+            (dispatch, 0), (dispatch, 1), (lay_weights, 0), (dispatched, 0), (dispatch, 2),
+            (spread, 0), (multiply, 0), (dispatched, 1), (dispatch, 3), (add_cores, 0),
+            (spread, 1), (multiply, 1), (add_cores, 1), (spread, 2), (multiply, 2), (add_cores, 2),
+            (add_columns, 0), (add_columns, 1), (add_columns, 2), (spread, 3), (multiply, 3),
+            (add_cores, 3), (add_columns, 3), (activate, 0), (gather, 0), (activate, 1),
+            (multiply_back, 0), (gather, 1), (add_halves, 0), (activate, 2), (multiply_back, 1),
+            (give_back, 0), (gather, 2), (add_halves, 1), (activate, 3), (multiply_back, 2),
+            (give_back, 1), (gather, 3), (add_halves, 2), (give_back, 2), (multiply_back, 3),
+            (add_halves, 3), (give_back, 3),
+        )
+        for stage, chunk in order:
+            stage(chunk)
 
         rows_all = held[...].reshape(CHUNKS * rows, 2 * width)
         for h in range(2):
@@ -230,11 +269,12 @@
             gu = dot(rows_all[:, 0:512], grads[:, 256:768], TN).astype(BF)
             gate_grad[:, 256 * h : 256 * h + 256] = gu[0:width, 0:256]
             up_grad[:, 256 * h : 256 * h + 256] = gu[0:width, 256:512]
-            down_grad[256 * h : 256 * h + 256, :] = dot(grads[:, 0:256], rows_all[:, low:], TN).astype(BF)
+            down = dot(rows_all[:, low:], grads[:, 0:256], TN).astype(BF)
+            down_grad[:, 256 * h : 256 * h + 256] = down[512 - width :, :]
 
         for cp in zb:
             cp.wait_recv()
-        token_grad[...] = dot(placing[...], ret[...].reshape(n_slot, width), TN).astype(BF)
+        token_grad[...] = dot(ret[...].reshape(n_slot, width), placing[...], TN).astype(BF)
         for cp in sent:
             cp.wait_send()
 
@@ -249,14 +289,6 @@
     span = group * CAP
     rows = NX * span
     n_slot = 2 * nz * CAP
-    pad = 512 - width
-    xg = jnp.concatenate([tokens, output_grad], axis=1)
-    halves = [
-        jnp.concatenate([gate_weight[0, :, h : h + 256], up_weight[0, :, h : h + 256]], axis=1)
-        for h in (0, 256)
-    ]
-    w3 = jnp.pad(jnp.stack(halves), ((0, 0), (0, pad), (0, 0)))
-    wd3 = jnp.pad(down_weight[0], ((0, 0), (pad, 0))).reshape(2, hidden // 2, 512)
     vmem = pl.BlockSpec(memory_space=pltpu.VMEM)
 
     def dma(*shape):
@@ -265,14 +297,17 @@
     token_grad, gate_grad, up_grad, down_grad = pl.pallas_call(
         make_kernel(nz, width),
         out_shape=(
-            jax.ShapeDtypeStruct(tokens.shape, BF),
+            jax.ShapeDtypeStruct(tokens.shape[::-1], BF),
             jax.ShapeDtypeStruct((width, hidden), BF),
             jax.ShapeDtypeStruct((width, hidden), BF),
-            jax.ShapeDtypeStruct((hidden, 512), BF),
+            jax.ShapeDtypeStruct((width, hidden), BF),
         ),
-        in_specs=[vmem] * 5,
+        in_specs=[vmem] * 7,
         out_specs=(vmem,) * 4,
         scratch_shapes=[
+            pltpu.VMEM((2 * width, tokens.shape[0]), BF),
+            pltpu.VMEM((2, 512, hidden), BF),
+            pltpu.VMEM((2, 512, hidden // 2), BF),
             pltpu.VMEM((n_slot, tokens.shape[0]), BF),
             pltpu.VMEM((nz, 2 * CAP, 2 * width), BF),
             pltpu.VMEM((nz, 2 * CAP, 2 * width), BF),
@@ -296,8 +331,11 @@
             collective_id=1, has_side_effects=True, vmem_limit_bytes=56 * 2**20
         ),
         name="layer",
-    )(expert_ids.T, route_weight.T, xg, w3, wd3)
-    return token_grad, gate_grad[None], up_grad[None], down_grad[None, :, pad:]
+    )(
+        expert_ids.T, route_weight.T, tokens.T, output_grad.T,
+        gate_weight[0], up_weight[0], down_weight[0].T,
+    )
+    return token_grad.T, gate_grad[None], up_grad[None], down_grad.T[None]
 
 
 def solution(mesh):

time: 230 us -> 197 us (0.86)
  the two profiles are of different devices: /device:TPU:98 before, /device:TPU:33 now
where the time goes in v2:
time: 197 us; the launch traced here: 196 us
  Pallas kernels  191 us (97%)
  local copies, waits for them, and re-layouts  4.83 us (2%)
    pallas_call x1, Pallas kernels, body(): pl.pallas_call(make_kernel(nz, width), out_shape=(jax.ShapeDtypeStruct(to...  191 us
    unnamed x10, local copies, waits for them, and re-layouts  4.83 us

profile of v2, /device:TPU:33, one launch (start us, length us, event | category | flops | bytes accessed | tf_op | source)
XLA Modules:
  0.0 196.4 jit_solution(1587759552946681895)
XLA Ops:
  0.6 190.9 %layer.1 = (bf16[448,256]{1,0:T(8,128)(2,1)}, bf16[448,512]{1,0:T(8,128)(2,1)}, bf16[448,512]{1,0:T(8,128)(2,1)}, bf16[448,512]{1,0:T(8,128)(2,1)}) custom-call(s32[8,256]{1,0:T(8,128)} %bitcast.24, f32[8,256]{1,0:T(8,128)} %bitcast.25, bf16[448,256]{1,0:T(8,128)(2,1)} %bitcast.21, bf16[448,256]{1,0:T(8,128)(2,1)} %bitcast.22, bf16[448,512]{1,0:T(8,128)(2,1)} %bitcast.15, ...), custom_call_target="tpu_custom_call" | custom-call | tf_op jit(solution)/shard_map/layer/pallas_call | solution.py:297
  191.5 0.0 copy-start.2
  191.6 1.7 copy.15
  193.3 0.0 copy-done.2
  193.3 0.0 copy-start.1
  193.3 0.8 copy.16
  194.0 0.4 copy-done.1
  194.4 0.0 copy-start
  194.4 0.8 copy.17
  195.2 0.4 copy-done
  195.6 0.8 copy.18
Async XLA Ops:
  191.5 1.7 copy-start.2
  193.3 1.2 copy-start.1
  194.4 1.2 copy-start

commit v3 on v2

--- a/solution.py
+++ b/solution.py
@@ -25,6 +25,18 @@
 
 def iota(shape, dim):
     return lax.broadcasted_iota(jnp.int32, shape, dim)
+
+
+def settle(a, b, c, d, a_out, b_out, c_out, d_out, sems):
+    copies = []
+    for i, (src, dst) in enumerate(((a, a_out), (b, b_out), (c, c_out), (d, d_out))):
+        rows = src.shape[0] // 4
+        for j in range(4):
+            part = pl.ds(j * rows, rows)
+            copies.append(pltpu.make_async_copy(src.at[part], dst.at[part], sems.at[i, j]))
+            copies[-1].start()
+    for copy in copies:
+        copy.wait()
 
 
 def make_kernel(nz, width):
@@ -294,7 +306,7 @@
     def dma(*shape):
         return [pltpu.SemaphoreType.DMA(shape)] * 2
 
-    token_grad, gate_grad, up_grad, down_grad = pl.pallas_call(
+    made = pl.pallas_call(
         make_kernel(nz, width),
         out_shape=(
             jax.ShapeDtypeStruct(tokens.shape[::-1], BF),
@@ -335,6 +347,14 @@
         expert_ids.T, route_weight.T, tokens.T, output_grad.T,
         gate_weight[0], up_weight[0], down_weight[0].T,
     )
+    token_grad, gate_grad, up_grad, down_grad = pl.pallas_call(
+        settle,
+        out_shape=[jax.ShapeDtypeStruct(m.shape, m.dtype) for m in made],
+        in_specs=[pl.BlockSpec(memory_space=pl.ANY)] * 4,
+        out_specs=[pl.BlockSpec(memory_space=pl.ANY)] * 4,
+        scratch_shapes=[pltpu.SemaphoreType.DMA((4, 4))],
+        name="settle",
+    )(*made)
     return token_grad.T, gate_grad[None], up_grad[None], down_grad.T[None]
 
 

time: 197 us -> 242 us (1.23)
  Pallas kernels: 191 us -> 241 us
  local copies, waits for them, and re-layouts: 4.83 us -> 0 us
    pallas_call x0 -> x1, Pallas kernels: none -> 49.9 us  [body(): pl.pallas_call(settle, out_shape=[jax.ShapeDtypeStruct(m.shape, m.dtype)...]
    unnamed x10 -> x0, local copies, waits for them, and re-layouts: 4.83 us -> none
where the time goes in v3:
time: 242 us; the launch traced here: 241 us
  Pallas kernels  241 us (100%)
    pallas_call x1, Pallas kernels, body(): pl.pallas_call(make_kernel(nz, width), out_shape=(jax.ShapeDtypeStruct(to...  191 us
    pallas_call x1, Pallas kernels, body(): pl.pallas_call(settle, out_shape=[jax.ShapeDtypeStruct(m.shape, m.dtype)...  49.9 us

profile of v3, /device:TPU:33, one launch (start us, length us, event | category | flops | bytes accessed | tf_op | source)
XLA Modules:
  0.0 241.4 jit_solution(15530526782351310267)
XLA Ops:
  0.6 190.9 %layer.1 = (bf16[448,256]{1,0:T(8,128)(2,1)}, bf16[448,512]{1,0:T(8,128)(2,1)}, bf16[448,512]{1,0:T(8,128)(2,1)}, bf16[448,512]{1,0:T(8,128)(2,1)}) custom-call(s32[8,256]{1,0:T(8,128)} %bitcast.20, f32[8,256]{1,0:T(8,128)} %bitcast.21, bf16[448,256]{1,0:T(8,128)(2,1)} %bitcast.18, bf16[448,256]{1,0:T(8,128)(2,1)} %bitcast.19, bf16[448,512]{1,0:T(8,128)(2,1)} %bitcast.15, ...), custom_call_target="tpu_custom_call" | custom-call | tf_op jit(solution)/shard_map/layer/pallas_call | solution.py:309
  191.6 49.9 %settle.1 = (bf16[448,256]{1,0:T(8,128)(2,1)}, bf16[448,512]{1,0:T(8,128)(2,1)}, bf16[448,512]{1,0:T(8,128)(2,1)}, bf16[448,512]{1,0:T(8,128)(2,1)}) custom-call(bf16[448,256]{1,0:T(8,128)(2,1)} %get-tuple-element.12.a, bf16[448,512]{1,0:T(8,128)(2,1)} %get-tuple-element.13.b, bf16[448,512]{1,0:T(8,128)(2,1)} %get-tuple-element.14.c, ...), custom_call_target="tpu_custom_call" | custom-call | tf_op jit(solution)/shard_map/settle/pallas_call | solution.py:350

commit v4 on v2

--- a/solution.py
+++ b/solution.py
@@ -25,6 +25,11 @@
 
 def iota(shape, dim):
     return lax.broadcasted_iota(jnp.int32, shape, dim)
+
+
+def settle(a, b, c, d, a_out, b_out, c_out, d_out):
+    for src, dst in ((a, a_out), (b, b_out), (c, c_out), (d, d_out)):
+        dst[...] = src[...]
 
 
 def make_kernel(nz, width):
@@ -294,7 +299,7 @@
     def dma(*shape):
         return [pltpu.SemaphoreType.DMA(shape)] * 2
 
-    token_grad, gate_grad, up_grad, down_grad = pl.pallas_call(
+    made = pl.pallas_call(
         make_kernel(nz, width),
         out_shape=(
             jax.ShapeDtypeStruct(tokens.shape[::-1], BF),
@@ -335,6 +340,13 @@
         expert_ids.T, route_weight.T, tokens.T, output_grad.T,
         gate_weight[0], up_weight[0], down_weight[0].T,
     )
+    token_grad, gate_grad, up_grad, down_grad = pl.pallas_call(
+        settle,
+        out_shape=[jax.ShapeDtypeStruct(m.shape, m.dtype) for m in made],
+        in_specs=[vmem] * 4,
+        out_specs=[vmem] * 4,
+        name="settle",
+    )(*made)
     return token_grad.T, gate_grad[None], up_grad[None], down_grad.T[None]
 
 

time: 197 us -> 194 us (0.985)
  local copies, waits for them, and re-layouts: 4.83 us -> 0 us
  Pallas kernels: 191 us -> 194 us
    unnamed x10 -> x0, local copies, waits for them, and re-layouts: 4.83 us -> none
    pallas_call x0 -> x1, Pallas kernels: none -> 2.58 us  [body(): pl.pallas_call(settle, out_shape=[jax.ShapeDtypeStruct(m.shape, m.dtype)...]
where the time goes in v4:
time: 194 us
  Pallas kernels  194 us (100%)
    pallas_call x1, Pallas kernels, body(): pl.pallas_call(make_kernel(nz, width), out_shape=(jax.ShapeDtypeStruct(to...  191 us

profile of v4, /device:TPU:33, one launch (start us, length us, event | category | flops | bytes accessed | tf_op | source)
XLA Modules:
  0.0 194.1 jit_solution(12467075644341416515)
XLA Ops:
  0.6 190.9 %layer.1 = (bf16[448,256]{1,0:T(8,128)(2,1)}, bf16[448,512]{1,0:T(8,128)(2,1)}, bf16[448,512]{1,0:T(8,128)(2,1)}, bf16[448,512]{1,0:T(8,128)(2,1)}) custom-call(s32[8,256]{1,0:T(8,128)} %bitcast.20, f32[8,256]{1,0:T(8,128)} %bitcast.21, bf16[448,256]{1,0:T(8,128)(2,1)} %bitcast.18, bf16[448,256]{1,0:T(8,128)(2,1)} %bitcast.19, bf16[448,512]{1,0:T(8,128)(2,1)} %bitcast.15, ...), custom_call_target="tpu_custom_call" | custom-call | tf_op jit(solution)/shard_map/layer/pallas_call | solution.py:302
  191.6 2.6 %settle.1 = (bf16[448,256]{1,0:T(8,128)(2,1)}, bf16[448,512]{1,0:T(8,128)(2,1)}, bf16[448,512]{1,0:T(8,128)(2,1)}, bf16[448,512]{1,0:T(8,128)(2,1)}) custom-call(bf16[448,256]{1,0:T(8,128)(2,1)} %get-tuple-element.12.a, bf16[448,512]{1,0:T(8,128)(2,1)} %get-tuple-element.13.b, bf16[448,512]{1,0:T(8,128)(2,1)} %get-tuple-element.14.c, ...), custom_call_target="tpu_custom_call" | custom-call | tf_op jit(solution)/shard_map/settle/pallas_call | solution.py:343
